TPU v7x, 512 devices: a whole 4x8x8 slice. The times are simulated.
512 devices in a mesh: tok: 64 (over y_hi, x, z), head: 8 (over y_lo, core).
Axes of the slice: x: 4, y: 8 (y_hi: 2, y_lo: 4; y = y_hi * 4 + y_lo), z: 8, core: 2. Of those that a mesh axis runs over, the one named last changes fastest.
Arguments:
- context: bfloat16 [8, 16384, 1024], P(None, 'tok'), may hold values from -6 to 6
- ctx_gain: float32 [1024], replicated, may hold values from 0.1 to 1.9
- queries: bfloat16 [64, 512], P('tok', 'head'), may hold values from -110 to 110
- key_weight: bfloat16 [1024, 512], P(None, 'head'), may hold values from -0.1875 to 0.1875
- value_weight: bfloat16 [1024, 512], P(None, 'head'), may hold values from -0.1875 to 0.1875
- out_weight: bfloat16 [512, 4096], P('head', 'tok'), may hold values from -0.25 to 0.25
Outputs:
- latent_out: bfloat16 [64, 8, 4096], P('head', None, 'tok')
All inputs are finite; a program needn't handle non-finite values.
Results may differ from a plain program's by a relative error of at most 0.0059.
The roundings to bfloat16 on the way count: a program that leaves them out, or rounds other values in their place, can miss the bound.
Values may be sent and summed in bfloat16 or wider, within the bound.
A program may use at most 64 MiB of HBM per device.

v0:
```python
import jax
import jax.numpy as jnp
from jax import lax
from jax.sharding import PartitionSpec as P

HD = 64


def joined(part, axis, combine):
    gathered = jax.tree.map(lambda a: lax.all_gather(a, axis), part)

    def take(source):
        return jax.tree.map(lambda a: lax.dynamic_index_in_dim(a, source, 0, False), gathered)

    return lax.fori_loop(
        1, lax.axis_size(axis), lambda source, state: combine(state, take(source)), take(0)
    )


def combine_parts(first, second):
    top = jnp.maximum(first[0], second[0])
    fa = jnp.exp(first[0] - top)
    fb = jnp.exp(second[0] - top)
    wide_a = jnp.repeat(fa, HD, axis=-1)
    wide_b = jnp.repeat(fb, HD, axis=-1)
    return (top, first[1] * fa + second[1] * fb, first[2] * wide_a + second[2] * wide_b)


def per_device(context, ctx_gain, queries, key_weight, value_weight, out_weight):
    all_queries = lax.all_gather(queries, "tok", axis=0, tiled=True)
    latents = all_queries.shape[0]
    width = key_weight.shape[1]
    nheads = width // HD
    videos = context.shape[0]
    tokens = context.shape[1]
    data = context.astype(jnp.float32)
    meansq = jnp.mean(data * data, axis=-1, keepdims=True)
    normed = (data * lax.rsqrt(meansq + 1e-06) * ctx_gain).astype(jnp.bfloat16)
    keys = jnp.dot(normed, key_weight, preferred_element_type=jnp.float32).astype(jnp.bfloat16)
    values = jnp.dot(normed, value_weight, preferred_element_type=jnp.float32).astype(jnp.bfloat16)
    scores = jnp.einsum(
        "lhd,vthd->vhlt",
        all_queries.reshape(latents, nheads, HD),
        keys.reshape(videos, tokens, nheads, HD),
        preferred_element_type=jnp.float32,
    ) * HD ** (-0.5)
    block_max = jnp.max(scores, axis=-1)
    expo = jnp.exp(scores - block_max[..., None])
    block_sum = jnp.transpose(jnp.sum(expo, axis=-1), (2, 0, 1))
    weights = expo.astype(jnp.bfloat16)
    block_acc = jnp.einsum(
        "vhlt,vthd->lvhd",
        weights,
        values.reshape(videos, tokens, nheads, HD),
        preferred_element_type=jnp.float32,
    ).reshape(latents, videos, width)
    block_max = jnp.transpose(block_max, (2, 0, 1))
    top, total, accum = joined((block_max, block_sum, block_acc), "tok", combine_parts)
    attended = (accum / jnp.repeat(total, HD, axis=-1)).astype(jnp.bfloat16)
    own_rows = latents // lax.axis_size("head")
    rows_part = attended.reshape(lax.axis_size("head") * own_rows * videos, width)
    product = jnp.dot(rows_part, out_weight, preferred_element_type=jnp.float32)
    summed = lax.psum_scatter(
        product.reshape(lax.axis_size("head") * own_rows, videos, out_weight.shape[1]),
        "head",
        scatter_dimension=0,
        tiled=True,
    )
    return summed.astype(jnp.bfloat16)


def solution(mesh):
    in_specs = (
        P(None, "tok", None),
        P(),
        P("tok", "head"),
        P(None, "head"),
        P(None, "head"),
        P("head", "tok"),
    )
    out_specs = P("head", None, "tok")
    return jax.shard_map(
        per_device, mesh=mesh, in_specs=in_specs, out_specs=out_specs, check_vma=False
    )
```

profile of v0, /device:TPU:1, one launch (start us, length us, event | category | flops | bytes accessed | tf_op | source)
XLA Modules:
  0.0 891.2 jit_solution(15301389529886321620)
XLA Ops:
  6.5 3.1 fusion.1
  9.7 200.9 %all-gather.3 = bf16[64,1,64]{2,1,0:T(2,128)(2,1)S(1)} all-gather(bf16[1,1,64]{2,1,0:T(2,128)(2,1)} %bitcast.98), channel_id=1, replica_groups=mesh['tok'=64,'head'=8] {'tok'}, dimensions={0}, use_global_device_ids=true | all-gather | bytes 8320 | tf_op jit(solution)/shard_map/all_gather | solution.py:30
  210.6 3.9 fusion.33
  214.5 3.5 convolution_bitcast_fusion
  219.4 230.7 %all-gather = f32[4096,8,1]{1,2,0:T(1,128)S(1)} all-gather(f32[64,8,1]{1,2,0:T(1,128)S(1)} %copy.53), channel_id=2, replica_groups=mesh['tok'=64,'head'=8] {'tok'}, dimensions={0}, use_global_device_ids=true | all-gather | bytes 133120 | tf_op jit(solution)/shard_map/all_gather | solution.py:10
  450.8 223.1 %all-gather.1 = f32[4096,8,1]{1,2,0:T(1,128)S(1)} all-gather(f32[64,8,1]{1,2,0:T(1,128)S(1)} %copy.54), channel_id=3, replica_groups=mesh['tok'=64,'head'=8] {'tok'}, dimensions={0}, use_global_device_ids=true | all-gather | bytes 133120 | tf_op jit(solution)/shard_map/all_gather | solution.py:10
  675.5 90.4 %while.22 = (s32[]{:T(128)}, f32[64,8,1]{0,2,1:T(1,128)S(1)}, f32[64,8,1]{0,2,1:T(1,128)S(1)}, f32[64,8,64]{2,1,0:T(8,128)S(1)}, f32[64,64,8,1]{1,2,3,0:T(8,128)...) while((s32[]{:T(128)}, f32[64,8,1]{0,2,1:T(1,128)S(1)}, ...), condition=%wide.region_4.5_spmd, body=%wide.region_3.4_spmd.sunk | while | flops 101381 | bytes 430223 | solution.py:15
  675.7 1.2 fusion.39
  677.1 1.2 fusion.39
  678.6 1.2 fusion.39
  680.0 1.2 fusion.39
  681.4 1.2 fusion.39
  682.9 1.2 fusion.39
  684.3 1.2 fusion.39
  685.7 1.2 fusion.39
  687.2 1.2 fusion.39
  688.6 1.2 fusion.39
  694.4 1.2 fusion.39
  703.0 1.2 fusion.39
  721.6 1.2 fusion.39
  730.2 1.2 fusion.39
  748.9 1.2 fusion.39
  757.5 1.2 fusion.39
  767.0 116.0 %reduce-scatter.2.cloned.1.call-done = f32[8,8,64]{2,0,1:T(8,128)} async-done(((f32[64,8,64]{2,0,1:T(8,128)}), f32[8,8,64]{2,0,1:T(8,128)}) %reduce-scatter.2.cloned.1.call-update) | async-done | bytes 16400 | tf_op jit(solution)/shard_map/reduce_scatter | solution.py:63
  (329 shorter events, 74.8 us)
Async XLA Ops:
  6.5 204.1 %copy-start = (bf16[1024,64]{0,1:T(8,128)(2,1)S(1)}, bf16[1024,64]{0,1:T(8,128)(2,1)}, u32[]{:S(2)}) copy-start(bf16[1024,64]{0,1:T(8,128)(2,1)} %param.11) | copy-start | bytes 393220
  6.5 208.0 %copy-start.3 = (f32[1024]{0:T(1024)S(1)}, f32[1024]{0:T(1024)}, u32[]{:S(2)}) copy-start(f32[1024]{0:T(1024)} %param.9) | copy-start | bytes 12292
  6.5 208.0 %copy-start.2 = (bf16[1024,64]{0,1:T(8,128)(2,1)S(1)}, bf16[1024,64]{0,1:T(8,128)(2,1)}, u32[]{:S(2)}) copy-start(bf16[1024,64]{0,1:T(8,128)(2,1)} %param.12) | copy-start | bytes 393220
  6.5 668.0 %all-gather.6.cloned.1.call-start = ((), (), s32[]{:S(2)}) async-start(), calls=%async_computation.2 | async-start | bytes 17039360 | tf_op jit(solution)/shard_map/all_gather | solution.py:10
  218.1 548.0 %copy-start.1 = (bf16[64,64]{1,0:T(8,128)(2,1)S(1)}, bf16[64,64]{1,0:T(8,128)(2,1)}, u32[]{:S(2)}) copy-start(bf16[64,64]{1,0:T(8,128)(2,1)} %param.13) | copy-start | bytes 24580
  218.9 664.0 %reduce-scatter.2.cloned.1.call-start = ((), (), s32[]{:S(2)}) async-start(), calls=%async_computation.1 | async-start | bytes 294912 | tf_op jit(solution)/shard_map/reduce_scatter | solution.py:63
Sparse Core Ops, SparseCore 0:
  219.1 317.5 all-gather.5
  767.1 115.8 reduce-scatter.1
where the time goes:
time: 895 us; the launch traced here: 891 us
  blocking collectives  655 us (73%)
  waiting for transfers between devices  116 us (13%)
  other arithmetic  81.1 us (9%)
  local copies, waits for them, and re-layouts  15.2 us (2%)
  between operations  13.5 us (2%)
    all_gather x2, blocking collectives, joined(): gathered = jax.tree.map(lambda a: lax.all_gather(a, axis), part)  454 us
    all_gather x1, blocking collectives, per_device(): all_queries = lax.all_gather(queries, 'tok', axis=0, tiled=True)  201 us
    reduce_scatter x1, waiting for transfers between devices, per_device(): lax.psum_scatter(product.reshape(lax.axis_size('head') * own_rows, videos...  116 us
    add x63, other arithmetic, combine_parts(): first[2] * wide_a + second[2] * wide_b  76 us
  transfers between devices with their start and end apart: 2, of which 1 were waited for; matrix products, arithmetic and copies ran while one was open for 0% of the time, Pallas kernels for 0%

commit v1 on v0

v1 whole, which is shorter than its diff:
```python
import functools

import jax
import jax.numpy as jnp
from jax import lax
from jax.experimental import pallas as pl
from jax.experimental.pallas import tpu as pltpu
from jax.sharding import PartitionSpec as P

MESH = pl.DeviceIdType.MESH
HD = 64
GROUP = 16
RING = (2, 4, 8)
HOPS = (4, 1, 1)
OPPOSITE = (1, 2, 4)


def distance(k):
    return sum(min(a, n - a) * w for a, n, w in zip(k, RING, HOPS))


def opposite(k):
    return tuple((o - a) % n for o, a, n in zip(OPPOSITE, k, RING))


def ordered_offsets():
    every = [(a, b, c) for a in range(2) for b in range(4) for c in range(8)]
    half = []
    for k in sorted(every, key=lambda k: (distance(k), k)):
        if len(half) < 32 and opposite(k) not in half:
            half.append(k)
    return half + [opposite(k) for k in reversed(half)]


OFFSETS = ordered_offsets()
N = len(OFFSETS)


def kernel(
    ctx, gain, query, key_t, value_t, out_w, out,
    xbuf, gbuf, qin, wt, w, normed, kv, qs, qr, ps, pr, att, ar, wr,
    in_sem, x_sem, q_send, q_recv, p_send, p_recv, a_send, a_recv, w_send, w_recv, w_own,
):
    tok, head = lax.axis_index("tok"), lax.axis_index("head")
    yh, x, z = tok // 32, (tok // 8) % 4, tok % 8
    ys = [((yh + a) % 2) * 32 for a in range(2)]
    xs = [((x + a) % 4) * 8 for a in range(4)]
    zs = [(z + a) % 8 for a in range(8)]

    def at(k):
        return ys[k[0]] + xs[k[1]] + zs[k[2]]

    videos = ctx.shape[0]
    small = [
        pltpu.make_async_copy(query, qin, in_sem.at[0]),
        pltpu.make_async_copy(value_t, wt.at[pl.ds(0, HD)], in_sem.at[1]),
        pltpu.make_async_copy(key_t, wt.at[pl.ds(HD, HD)], in_sem.at[2]),
        pltpu.make_async_copy(gain, gbuf, in_sem.at[3]),
    ]
    big = [pltpu.make_async_copy(ctx.at[v], xbuf.at[v], x_sem.at[v]) for v in range(videos)]
    for copy in small:
        copy.start()
    big[0].start()
    barrier = pltpu.get_barrier_semaphore()
    for k in reversed(OFFSETS[1:]):
        pl.semaphore_signal(barrier, inc=1, device_id={"tok": at(k), "head": head}, device_id_type=MESH)
    for i in range(1, 8):
        pl.semaphore_signal(barrier, inc=1, device_id={"tok": tok, "head": (head + i) % 8}, device_id_type=MESH)
    for copy in big[1:]:
        copy.start()
    own_w = pltpu.make_async_copy(out_w, wr.at[head], w_own)
    own_w.start()

    for copy in small:
        copy.wait()
    row = qin[...].astype(jnp.float32) * HD**-0.5
    row = jnp.concatenate([jnp.zeros((1, HD), jnp.float32), row], axis=1)
    qs[0] = row
    qr[0] = row
    w[...] = wt[...].T

    for v in range(videos):
        big[v].wait()
        data = xbuf[v].astype(jnp.float32)
        meansq = jnp.mean(data * data, axis=-1, keepdims=True)
        normed[...] = (data * lax.rsqrt(meansq + 1e-06) * gbuf[...]).astype(jnp.bfloat16)
        kv[v] = jnp.dot(normed[...], w[...], preferred_element_type=jnp.float32).astype(jnp.bfloat16)

    pl.semaphore_wait(barrier, N - 1 + 7)
    for j in reversed(range(1, N)):
        pltpu.make_async_remote_copy(
            src_ref=qs.at[0], dst_ref=qr.at[j], send_sem=q_send, recv_sem=q_recv.at[j // GROUP],
            device_id={"tok": at(OFFSETS[j]), "head": head}, device_id_type=MESH,
        ).start()
    for i in range(1, 8):
        pltpu.make_async_remote_copy(
            src_ref=out_w, dst_ref=wr.at[head], send_sem=w_send, recv_sem=w_recv,
            device_id={"tok": tok, "head": (head + i) % 8}, device_id_type=MESH,
        ).start()

    lane = lax.broadcasted_iota(jnp.int32, (GROUP, 2 * HD), 1)
    for g in range(N // GROUP):
        first = max(g * GROUP, 1)
        came = qr.at[pl.ds(first, (g + 1) * GROUP - first)]
        pltpu.make_async_copy(came, came, q_recv.at[g]).wait()
        rows = pl.ds(g * GROUP, GROUP)
        qg = qr[rows].reshape(GROUP, 2 * HD).astype(jnp.bfloat16)
        for v in range(videos):
            scores = lax.dot_general(qg, kv[v], (((1,), (1,)), ((), ())), preferred_element_type=jnp.float32)
            top = jnp.max(scores, axis=-1, keepdims=True)
            expo = jnp.exp(scores - top)
            total = jnp.sum(expo, axis=-1, keepdims=True)
            acc = jnp.dot(expo.astype(jnp.bfloat16), kv[v], preferred_element_type=jnp.float32)
            ps[rows, v, :] = jnp.where(lane < HD, acc, jnp.where(lane == HD, top, total))
        for j in range(g * GROUP, (g + 1) * GROUP):
            if j < N - 1:
                pltpu.make_async_remote_copy(
                    src_ref=ps.at[j], dst_ref=pr.at[j], send_sem=p_send, recv_sem=p_recv,
                    device_id={"tok": at(opposite(OFFSETS[j])), "head": head}, device_id_type=MESH,
                ).start()
            else:
                pr[j] = ps[j]

    came = pr.at[pl.ds(0, N - 1)]
    pltpu.make_async_copy(came, came, p_recv).wait()
    parts = pr[...]
    top = jnp.max(parts, axis=0)
    factor = jnp.exp(parts - top[None])[:, :, HD : HD + 1]
    joined = jnp.sum(parts * factor, axis=0)
    att[...] = joined / joined[:, HD + 1 : HD + 2]

    mine = ((yh + 1) % 2) * 4 + (x + 2) % 4
    slot = (z + 4) % 8
    for j in reversed(range(1, N)):
        pltpu.make_async_remote_copy(
            src_ref=att, dst_ref=ar.at[head, slot], send_sem=a_send, recv_sem=a_recv,
            device_id={"tok": at(OFFSETS[j]), "head": mine}, device_id_type=MESH,
        ).start()

    @pl.when(mine != head)
    def _():
        pltpu.make_async_remote_copy(
            src_ref=att, dst_ref=ar.at[head, slot], send_sem=a_send, recv_sem=a_recv,
            device_id={"tok": tok, "head": mine}, device_id_type=MESH,
        ).start()

    @pl.when(mine == head)
    def _():
        pltpu.make_async_copy(att, ar.at[head, slot], a_recv).start()

    own_w.wait()
    pltpu.make_async_copy(wr.at[pl.ds(0, 7)], wr.at[pl.ds(0, 7)], w_recv).wait()
    pltpu.make_async_copy(wr.at[pl.ds(0, 7)], wr.at[pl.ds(0, 7)], w_send).wait()
    gone = qr.at[pl.ds(0, N - 1)]
    pltpu.make_async_copy(gone, gone, q_send).wait()
    gone = ps.at[pl.ds(0, N - 1)]
    pltpu.make_async_copy(gone, gone, p_send).wait()

    pltpu.make_async_copy(ar, ar, a_recv).wait()
    result = jnp.zeros((64, HD), jnp.float32)
    for h in range(8):
        attended = ar[h].reshape(64, 2 * HD)[:, :HD].astype(jnp.bfloat16)
        result += jnp.dot(attended, wr[h], preferred_element_type=jnp.float32)
    out[...] = result.reshape(out.shape).astype(out.dtype)

    pltpu.make_async_copy(gone, gone, a_send).wait()

    @pl.when(mine != head)
    def _():
        pltpu.make_async_copy(att, att, a_send).wait()


def per_device(context, ctx_gain, queries, key_weight, value_weight, out_weight):
    videos, tokens, width = context.shape
    f32, bf16 = jnp.float32, jnp.bfloat16
    anywhere = pl.BlockSpec(memory_space=pl.ANY)
    dma = pltpu.SemaphoreType.DMA
    return pl.pallas_call(
        kernel,
        out_shape=jax.ShapeDtypeStruct((8, videos, out_weight.shape[1]), bf16),
        in_specs=[anywhere] * 6,
        out_specs=pl.BlockSpec(memory_space=pltpu.VMEM),
        scratch_shapes=[
            pltpu.VMEM((videos, tokens, width), bf16),
            pltpu.VMEM((1, width), f32),
            pltpu.VMEM((1, HD), bf16),
            pltpu.VMEM((2 * HD, width), bf16),
            pltpu.VMEM((width, 2 * HD), bf16),
            pltpu.VMEM((tokens, width), bf16),
            pltpu.VMEM((videos, tokens, 2 * HD), bf16),
            pltpu.VMEM((1, 1, 2 * HD), f32),
            pltpu.VMEM((N, 1, 2 * HD), f32),
            pltpu.VMEM((N, videos, 2 * HD), f32),
            pltpu.VMEM((N, videos, 2 * HD), f32),
            pltpu.VMEM((videos, 2 * HD), f32),
            pltpu.VMEM((8, 8, videos, 2 * HD), f32),
            pltpu.VMEM((8, HD, out_weight.shape[1]), bf16),
            dma((4,)), dma((videos,)),
            dma, dma((N // GROUP,)), dma, dma, dma, dma, dma, dma, dma,
        ],
        compiler_params=pltpu.CompilerParams(
            collective_id=0, has_side_effects=True, vmem_limit_bytes=40 * 2**20
        ),
        name="resampler",
    )(context, ctx_gain.reshape(1, width), queries, key_weight.T, value_weight.T, out_weight)


def solution(mesh):
    in_specs = (
        P(None, "tok", None),
        P(),
        P("tok", "head"),
        P(None, "head"),
        P(None, "head"),
        P("head", "tok"),
    )
    out_specs = P("head", None, "tok")
    return jax.shard_map(per_device, mesh=mesh, in_specs=in_specs, out_specs=out_specs, check_vma=False)
```

time: 895 us -> 65.3 us (0.07)
  the two profiles are of different devices: /device:TPU:1 before, /device:TPU:57 now
where the time goes in v1:
time: 65.3 us; the launch traced here: 65 us
  Pallas kernels  58.4 us (89%)
  local copies, waits for them, and re-layouts  6.66 us (10%)
    pallas_call x1, Pallas kernels, per_device(): pl.pallas_call(kernel, out_shape=jax.ShapeDtypeStruct((8, videos, out_wei...  58.4 us
    unnamed x13, local copies, waits for them, and re-layouts  6.66 us

profile of v1, /device:TPU:57, one launch (start us, length us, event | category | flops | bytes accessed | tf_op | source)
XLA Modules:
  0.0 65.0 jit_solution(12557995901654690919)
XLA Ops:
  0.0 0.0 copy-start
  0.0 2.2 %copy-done = bf16[8,256,1024]{2,1,0:T(8,128)(2,1)S(1)} copy-done((bf16[8,256,1024]{2,1,0:T(8,128)(2,1)S(1)}, bf16[8,256,1024]{2,1,0:T(8,128)(2,1)}, u32[]{:S(2)}) %copy-start) | copy-done | bytes 4194328
  2.2 0.0 copy-start.1
  2.2 0.9 %copy-done.1 = bf16[1024,64]{0,1:T(8,128)(2,1)S(1)} copy-done((bf16[1024,64]{0,1:T(8,128)(2,1)S(1)}, bf16[1024,64]{0,1:T(8,128)(2,1)}, u32[]{:S(2)}) %copy-start.1) | copy-done | bytes 131096
  3.1 0.0 copy-start.2
  3.1 0.9 %copy-done.2 = bf16[1024,64]{0,1:T(8,128)(2,1)S(1)} copy-done((bf16[1024,64]{0,1:T(8,128)(2,1)S(1)}, bf16[1024,64]{0,1:T(8,128)(2,1)}, u32[]{:S(2)}) %copy-start.2) | copy-done | bytes 131096
  4.0 0.0 copy-start.3
  4.0 0.7 %copy-done.3 = bf16[64,64]{1,0:T(8,128)(2,1)S(1)} copy-done((bf16[64,64]{1,0:T(8,128)(2,1)S(1)}, bf16[64,64]{1,0:T(8,128)(2,1)}, u32[]{:S(2)}) %copy-start.3) | copy-done | bytes 8216
  4.7 0.0 copy-start.4
  4.7 0.7 %copy-done.4 = f32[1024]{0:T(1024)S(1)} copy-done((f32[1024]{0:T(1024)S(1)}, f32[1024]{0:T(1024)}, u32[]{:S(2)}) %copy-start.4) | copy-done | bytes 4120
  5.4 0.0 copy-start.5
  5.4 0.7 %copy-done.5 = bf16[1,64]{1,0:T(2,128)(2,1)S(1)} copy-done((bf16[1,64]{1,0:T(2,128)(2,1)S(1)}, bf16[1,64]{1,0:T(2,128)(2,1)}, u32[]{:S(2)}) %copy-start.5) | copy-done | bytes 152
  6.1 58.4 %resampler.1 = bf16[8,8,64]{2,1,0:T(8,128)(2,1)S(1)} custom-call(bf16[8,256,1024]{2,1,0:T(8,128)(2,1)S(1)} %copy-done, f32[1,1024]{1,0:T(1,128)S(1)} %bitcast.5, bf16[1,64]{1,0:T(2,128)(2,1)S(1)} %copy-done.5, bf16[64,1024]{1,0:T(8,128)(2,1)S(1)} %bitcast.3, bf16[64,1024]{1,0:T(8,128)(2,1)S(1)} %bitcast.4, bf16[64,64]{1,0:T(8,128)(2,1)S(1)} %copy-done.3), custom_call_target="tpu_custom_call" | custom-call | tf_op jit(solution)/shard_map/resampler/pallas_call | solution.py:178
  64.4 0.6 copy.8
Async XLA Ops:
  0.0 2.2 %copy-start = (bf16[8,256,1024]{2,1,0:T(8,128)(2,1)S(1)}, bf16[8,256,1024]{2,1,0:T(8,128)(2,1)}, u32[]{:S(2)}) copy-start(bf16[8,256,1024]{2,1,0:T(8,128)(2,1)} %ctx.1) | copy-start | bytes 12582916
  2.2 0.9 %copy-start.1 = (bf16[1024,64]{0,1:T(8,128)(2,1)S(1)}, bf16[1024,64]{0,1:T(8,128)(2,1)}, u32[]{:S(2)}) copy-start(bf16[1024,64]{0,1:T(8,128)(2,1)} %param.9) | copy-start | bytes 393220
  3.1 0.9 %copy-start.2 = (bf16[1024,64]{0,1:T(8,128)(2,1)S(1)}, bf16[1024,64]{0,1:T(8,128)(2,1)}, u32[]{:S(2)}) copy-start(bf16[1024,64]{0,1:T(8,128)(2,1)} %param.10) | copy-start | bytes 393220
  4.0 0.7 %copy-start.3 = (bf16[64,64]{1,0:T(8,128)(2,1)S(1)}, bf16[64,64]{1,0:T(8,128)(2,1)}, u32[]{:S(2)}) copy-start(bf16[64,64]{1,0:T(8,128)(2,1)} %out_w.1) | copy-start | bytes 24580
  4.7 0.7 %copy-start.4 = (f32[1024]{0:T(1024)S(1)}, f32[1024]{0:T(1024)}, u32[]{:S(2)}) copy-start(f32[1024]{0:T(1024)} %param.7) | copy-start | bytes 12292
  5.4 0.7 %copy-start.5 = (bf16[1,64]{1,0:T(2,128)(2,1)S(1)}, bf16[1,64]{1,0:T(2,128)(2,1)}, u32[]{:S(2)}) copy-start(bf16[1,64]{1,0:T(2,128)(2,1)} %query.1) | copy-start | bytes 388

commit v2 on v1

--- a/solution.py
+++ b/solution.py
@@ -10,6 +10,7 @@
 MESH = pl.DeviceIdType.MESH
 HD = 64
 GROUP = 16
+HALF = 4
 RING = (2, 4, 8)
 HOPS = (4, 1, 1)
 OPPOSITE = (1, 2, 4)
@@ -38,7 +39,7 @@
 
 def kernel(
     ctx, gain, query, key_t, value_t, out_w, out,
-    xbuf, gbuf, qin, wt, w, normed, kv, qs, qr, ps, pr, att, ar, wr,
+    xbuf, gbuf, qin, wt, w, normed, kv, qs, qr, ps, pr, att, ar, wr, wd,
     in_sem, x_sem, q_send, q_recv, p_send, p_recv, a_send, a_recv, w_send, w_recv, w_own,
 ):
     tok, head = lax.axis_index("tok"), lax.axis_index("head")
@@ -53,8 +54,8 @@
     videos = ctx.shape[0]
     small = [
         pltpu.make_async_copy(query, qin, in_sem.at[0]),
-        pltpu.make_async_copy(value_t, wt.at[pl.ds(0, HD)], in_sem.at[1]),
-        pltpu.make_async_copy(key_t, wt.at[pl.ds(HD, HD)], in_sem.at[2]),
+        pltpu.make_async_copy(value_t, wt.at[0], in_sem.at[1]),
+        pltpu.make_async_copy(key_t, wt.at[1], in_sem.at[2]),
         pltpu.make_async_copy(gain, gbuf, in_sem.at[3]),
     ]
     big = [pltpu.make_async_copy(ctx.at[v], xbuf.at[v], x_sem.at[v]) for v in range(videos)]
@@ -77,14 +78,16 @@
     row = jnp.concatenate([jnp.zeros((1, HD), jnp.float32), row], axis=1)
     qs[0] = row
     qr[0] = row
-    w[...] = wt[...].T
+    value_w, key_w = wt[0].T, wt[1].T
+    w[0] = jnp.concatenate([value_w, key_w], axis=1)
+    w[1] = jnp.concatenate([key_w, value_w], axis=1)
 
     for v in range(videos):
         big[v].wait()
         data = xbuf[v].astype(jnp.float32)
         meansq = jnp.mean(data * data, axis=-1, keepdims=True)
         normed[...] = (data * lax.rsqrt(meansq + 1e-06) * gbuf[...]).astype(jnp.bfloat16)
-        kv[v] = jnp.dot(normed[...], w[...], preferred_element_type=jnp.float32).astype(jnp.bfloat16)
+        kv[v] = jnp.dot(normed[...], w[v // HALF], preferred_element_type=jnp.float32).astype(jnp.bfloat16)
 
     pl.semaphore_wait(barrier, N - 1 + 7)
     for j in reversed(range(1, N)):
@@ -104,14 +107,21 @@
         came = qr.at[pl.ds(first, (g + 1) * GROUP - first)]
         pltpu.make_async_copy(came, came, q_recv.at[g]).wait()
         rows = pl.ds(g * GROUP, GROUP)
-        qg = qr[rows].reshape(GROUP, 2 * HD).astype(jnp.bfloat16)
+        qg = qr[rows].reshape(GROUP, 2 * HD)
+        qs_of = [qg.astype(jnp.bfloat16), pltpu.roll(qg, HD, 1).astype(jnp.bfloat16)]
+        accs, stats = [], jnp.zeros((GROUP, 2 * HD), jnp.float32)
         for v in range(videos):
-            scores = lax.dot_general(qg, kv[v], (((1,), (1,)), ((), ())), preferred_element_type=jnp.float32)
+            scores = lax.dot_general(
+                qs_of[v // HALF], kv[v], (((1,), (1,)), ((), ())), preferred_element_type=jnp.float32
+            )
             top = jnp.max(scores, axis=-1, keepdims=True)
             expo = jnp.exp(scores - top)
             total = jnp.sum(expo, axis=-1, keepdims=True)
-            acc = jnp.dot(expo.astype(jnp.bfloat16), kv[v], preferred_element_type=jnp.float32)
-            ps[rows, v, :] = jnp.where(lane < HD, acc, jnp.where(lane == HD, top, total))
+            accs.append(jnp.dot(expo.astype(jnp.bfloat16), kv[v], preferred_element_type=jnp.float32))
+            stats = jnp.where(lane == v, top, jnp.where(lane == videos + v, total, stats))
+        for i in range(HALF):
+            ps[rows, i, :] = jnp.where(lane < HD, accs[i], accs[i + HALF])
+        ps[rows, HALF, :] = stats
         for j in range(g * GROUP, (g + 1) * GROUP):
             if j < N - 1:
                 pltpu.make_async_remote_copy(
@@ -121,13 +131,27 @@
             else:
                 pr[j] = ps[j]
 
+    own_w.wait()
+    pltpu.make_async_copy(wr.at[pl.ds(0, 7)], wr.at[pl.ds(0, 7)], w_recv).wait()
+    zeros = jnp.zeros((HD, HD), jnp.bfloat16)
+    for h in range(8):
+        wide = jnp.concatenate([wr[h], zeros], axis=1)
+        wd[pl.ds(2 * HD * h, HD)] = wide
+        wide = jnp.concatenate([zeros, wr[h]], axis=1)
+        wd[pl.ds(2 * HD * h + HD, HD)] = wide
+
     came = pr.at[pl.ds(0, N - 1)]
     pltpu.make_async_copy(came, came, p_recv).wait()
-    parts = pr[...]
-    top = jnp.max(parts, axis=0)
-    factor = jnp.exp(parts - top[None])[:, :, HD : HD + 1]
-    joined = jnp.sum(parts * factor, axis=0)
-    att[...] = joined / joined[:, HD + 1 : HD + 2]
+    stats = pr[:, HALF, :]
+    low = lax.broadcasted_iota(jnp.int32, (1, 2 * HD), 1) < HD
+    factor = jnp.exp(stats - jnp.max(stats, axis=0, keepdims=True))
+    total = jnp.sum(factor * pltpu.roll(stats, 2 * HD - videos, 1), axis=0, keepdims=True)
+    attended = []
+    for i in range(HALF):
+        weight = jnp.where(low, factor[:, i : i + 1], factor[:, i + HALF : i + HALF + 1])
+        accum = jnp.sum(weight * pr[:, i, :], axis=0, keepdims=True)
+        attended.append(accum / jnp.where(low, total[:, i : i + 1], total[:, i + HALF : i + HALF + 1]))
+    att[...] = jnp.concatenate(attended, axis=0).astype(att.dtype)
 
     mine = ((yh + 1) % 2) * 4 + (x + 2) % 4
     slot = (z + 4) % 8
@@ -148,8 +172,6 @@
     def _():
         pltpu.make_async_copy(att, ar.at[head, slot], a_recv).start()
 
-    own_w.wait()
-    pltpu.make_async_copy(wr.at[pl.ds(0, 7)], wr.at[pl.ds(0, 7)], w_recv).wait()
     pltpu.make_async_copy(wr.at[pl.ds(0, 7)], wr.at[pl.ds(0, 7)], w_send).wait()
     gone = qr.at[pl.ds(0, N - 1)]
     pltpu.make_async_copy(gone, gone, q_send).wait()
@@ -157,13 +179,14 @@
     pltpu.make_async_copy(gone, gone, p_send).wait()
 
     pltpu.make_async_copy(ar, ar, a_recv).wait()
-    result = jnp.zeros((64, HD), jnp.float32)
-    for h in range(8):
-        attended = ar[h].reshape(64, 2 * HD)[:, :HD].astype(jnp.bfloat16)
-        result += jnp.dot(attended, wr[h], preferred_element_type=jnp.float32)
-    out[...] = result.reshape(out.shape).astype(out.dtype)
-
-    pltpu.make_async_copy(gone, gone, a_send).wait()
+    blocks = [ar[h].astype(jnp.float32).reshape(8 * HALF, 2 * HD).astype(jnp.bfloat16) for h in range(8)]
+    result = jnp.dot(jnp.concatenate(blocks, axis=1), wd[...], preferred_element_type=jnp.float32)
+    result = result.reshape(8, HALF, 2 * HD)
+    out[...] = jnp.concatenate([result[:, :, :HD], result[:, :, HD:]], axis=1).astype(out.dtype)
+
+    gone = ar.at[0, pl.ds(0, 7)]
+    for _ in range(9):
+        pltpu.make_async_copy(gone, gone, a_send).wait()
 
     @pl.when(mine != head)
     def _():
@@ -184,22 +207,23 @@
             pltpu.VMEM((videos, tokens, width), bf16),
             pltpu.VMEM((1, width), f32),
             pltpu.VMEM((1, HD), bf16),
-            pltpu.VMEM((2 * HD, width), bf16),
-            pltpu.VMEM((width, 2 * HD), bf16),
+            pltpu.VMEM((2, HD, width), bf16),
+            pltpu.VMEM((2, width, 2 * HD), bf16),
             pltpu.VMEM((tokens, width), bf16),
             pltpu.VMEM((videos, tokens, 2 * HD), bf16),
             pltpu.VMEM((1, 1, 2 * HD), f32),
             pltpu.VMEM((N, 1, 2 * HD), f32),
-            pltpu.VMEM((N, videos, 2 * HD), f32),
-            pltpu.VMEM((N, videos, 2 * HD), f32),
-            pltpu.VMEM((videos, 2 * HD), f32),
-            pltpu.VMEM((8, 8, videos, 2 * HD), f32),
+            pltpu.VMEM((N, HALF + 1, 2 * HD), f32),
+            pltpu.VMEM((N, HALF + 1, 2 * HD), f32),
+            pltpu.VMEM((HALF, 2 * HD), bf16),
+            pltpu.VMEM((8, 8, HALF, 2 * HD), bf16),
             pltpu.VMEM((8, HD, out_weight.shape[1]), bf16),
+            pltpu.VMEM((8 * 2 * HD, 2 * HD), bf16),
             dma((4,)), dma((videos,)),
             dma, dma((N // GROUP,)), dma, dma, dma, dma, dma, dma, dma,
         ],
         compiler_params=pltpu.CompilerParams(
-            collective_id=0, has_side_effects=True, vmem_limit_bytes=40 * 2**20
+            collective_id=0, has_side_effects=True, vmem_limit_bytes=60 * 2**20
         ),
         name="resampler",
     )(context, ctx_gain.reshape(1, width), queries, key_weight.T, value_weight.T, out_weight)

time: 65.3 us -> 46.1 us (0.71)
  the two profiles are of different devices: /device:TPU:57 before, /device:TPU:1 now
where the time goes in v2:
time: 46.1 us; the launch traced here: 45.9 us
  Pallas kernels  44.5 us (97%)
  local copies, waits for them, and re-layouts  1.32 us (3%)
    pallas_call x1, Pallas kernels, per_device(): pl.pallas_call(kernel, out_shape=jax.ShapeDtypeStruct((8, videos, out_wei...  44.5 us
    unnamed x1, local copies, waits for them, and re-layouts  1.32 us

profile of v2, /device:TPU:1, one launch (start us, length us, event | category | flops | bytes accessed | tf_op | source)
XLA Modules:
  0.0 45.9 jit_solution(10410976094047288100)
XLA Ops:
  0.0 44.5 %resampler.1 = bf16[8,8,64]{2,1,0:T(8,128)(2,1)} custom-call(bf16[8,256,1024]{2,1,0:T(8,128)(2,1)} %ctx.1, f32[1,1024]{1,0:T(1,128)} %bitcast.5, bf16[1,64]{1,0:T(2,128)(2,1)} %query.1, bf16[64,1024]{1,0:T(8,128)(2,1)} %bitcast.3, bf16[64,1024]{1,0:T(8,128)(2,1)} %bitcast.4, bf16[64,64]{1,0:T(8,128)(2,1)} %out_w.1), custom_call_target="tpu_custom_call" | custom-call | tf_op jit(solution)/shard_map/resampler/pallas_call | solution.py:201
  44.5 1.3 %copy.8 = bf16[8,8,64]{2,1,0:T(8,128)(2,1)} copy(bf16[8,8,64]{2,1,0:T(8,128)(2,1)} %resampler.1) | data formatting | bytes 16384

commit v3 on v2

--- a/solution.py
+++ b/solution.py
@@ -9,7 +9,7 @@
 
 MESH = pl.DeviceIdType.MESH
 HD = 64
-GROUP = 16
+GROUP = 8
 HALF = 4
 RING = (2, 4, 8)
 HOPS = (4, 1, 1)
@@ -39,7 +39,7 @@
 
 def kernel(
     ctx, gain, query, key_t, value_t, out_w, out,
-    xbuf, gbuf, qin, wt, w, normed, kv, qs, qr, ps, pr, att, ar, wr, wd,
+    xbuf, gbuf, qin, wt, normed, keys_t, values, qs, qr, ps, pr, att, ar, wr, wd,
     in_sem, x_sem, q_send, q_recv, p_send, p_recv, a_send, a_recv, w_send, w_recv, w_own,
 ):
     tok, head = lax.axis_index("tok"), lax.axis_index("head")
@@ -75,19 +75,27 @@
     for copy in small:
         copy.wait()
     row = qin[...].astype(jnp.float32) * HD**-0.5
-    row = jnp.concatenate([jnp.zeros((1, HD), jnp.float32), row], axis=1)
+    row = jnp.concatenate([row, row], axis=1)
     qs[0] = row
     qr[0] = row
-    value_w, key_w = wt[0].T, wt[1].T
-    w[0] = jnp.concatenate([value_w, key_w], axis=1)
-    w[1] = jnp.concatenate([key_w, value_w], axis=1)
-
-    for v in range(videos):
+
+    key_value = jnp.concatenate([wt[1], wt[0]], axis=0)
+    value_key = jnp.concatenate([wt[0], wt[1]], axis=0)
+    low = lax.broadcasted_iota(jnp.int32, (xbuf.shape[1], 2 * HD), 1) < HD
+
+    def project(v, weights):
         big[v].wait()
         data = xbuf[v].astype(jnp.float32)
         meansq = jnp.mean(data * data, axis=-1, keepdims=True)
-        normed[...] = (data * lax.rsqrt(meansq + 1e-06) * gbuf[...]).astype(jnp.bfloat16)
-        kv[v] = jnp.dot(normed[...], w[v // HALF], preferred_element_type=jnp.float32).astype(jnp.bfloat16)
+        normed[v] = (data * lax.rsqrt(meansq + 1e-06) * gbuf[...]).astype(jnp.bfloat16)
+        return lax.dot_general(
+            normed[v], weights, (((1,), (1,)), ((), ())), preferred_element_type=jnp.float32
+        )
+
+    for i in range(HALF):
+        first, second = project(i, key_value), project(i + HALF, value_key)
+        keys_t[i] = jnp.where(low, first, second).astype(jnp.bfloat16).T
+        values[i] = jnp.where(low, second, first).astype(jnp.bfloat16)
 
     pl.semaphore_wait(barrier, N - 1 + 7)
     for j in reversed(range(1, N)):
@@ -102,25 +110,39 @@
         ).start()
 
     lane = lax.broadcasted_iota(jnp.int32, (GROUP, 2 * HD), 1)
+    all_keys_t = keys_t[...].reshape(HALF * 2 * HD, xbuf.shape[1])
+    all_values = jnp.concatenate([values[i] for i in range(HALF)], axis=1)
     for g in range(N // GROUP):
         first = max(g * GROUP, 1)
         came = qr.at[pl.ds(first, (g + 1) * GROUP - first)]
         pltpu.make_async_copy(came, came, q_recv.at[g]).wait()
         rows = pl.ds(g * GROUP, GROUP)
-        qg = qr[rows].reshape(GROUP, 2 * HD)
-        qs_of = [qg.astype(jnp.bfloat16), pltpu.roll(qg, HD, 1).astype(jnp.bfloat16)]
-        accs, stats = [], jnp.zeros((GROUP, 2 * HD), jnp.float32)
+        both = qr[rows].reshape(GROUP, 2 * HD)
+        left, right = jnp.where(lane < HD, both, 0.0), jnp.where(lane < HD, 0.0, both)
+        none = jnp.zeros_like(both)
+        spread = jnp.concatenate(
+            [
+                jnp.concatenate(
+                    [(left if v < HALF else right) if v % HALF == i else none for v in range(videos)], axis=0
+                )
+                for i in range(HALF)
+            ],
+            axis=1,
+        ).astype(jnp.bfloat16)
+        scores = jnp.dot(spread, all_keys_t, preferred_element_type=jnp.float32)
+        top = jnp.max(scores, axis=-1, keepdims=True)
+        expo = jnp.exp(scores - top)
+        total = jnp.sum(expo, axis=-1, keepdims=True)
+        acc = jnp.dot(expo.astype(jnp.bfloat16), all_values, preferred_element_type=jnp.float32)
+        stats = jnp.zeros((GROUP, 2 * HD), jnp.float32)
         for v in range(videos):
-            scores = lax.dot_general(
-                qs_of[v // HALF], kv[v], (((1,), (1,)), ((), ())), preferred_element_type=jnp.float32
-            )
-            top = jnp.max(scores, axis=-1, keepdims=True)
-            expo = jnp.exp(scores - top)
-            total = jnp.sum(expo, axis=-1, keepdims=True)
-            accs.append(jnp.dot(expo.astype(jnp.bfloat16), kv[v], preferred_element_type=jnp.float32))
-            stats = jnp.where(lane == v, top, jnp.where(lane == videos + v, total, stats))
+            own = slice(v * GROUP, (v + 1) * GROUP)
+            stats = jnp.where(lane == v, top[own], jnp.where(lane == videos + v, total[own], stats))
         for i in range(HALF):
-            ps[rows, i, :] = jnp.where(lane < HD, accs[i], accs[i + HALF])
+            lanes = slice(2 * HD * i, 2 * HD * (i + 1))
+            low_rows = slice((i + HALF) * GROUP, (i + HALF + 1) * GROUP)
+            high_rows = slice(i * GROUP, (i + 1) * GROUP)
+            ps[rows, i, :] = jnp.where(lane < HD, acc[low_rows, lanes], acc[high_rows, lanes])
         ps[rows, HALF, :] = stats
         for j in range(g * GROUP, (g + 1) * GROUP):
             if j < N - 1:
@@ -135,9 +157,9 @@
     pltpu.make_async_copy(wr.at[pl.ds(0, 7)], wr.at[pl.ds(0, 7)], w_recv).wait()
     zeros = jnp.zeros((HD, HD), jnp.bfloat16)
     for h in range(8):
+        wide = jnp.concatenate([zeros, wr[h]], axis=1)
+        wd[pl.ds(2 * HD * h, HD)] = wide
         wide = jnp.concatenate([wr[h], zeros], axis=1)
-        wd[pl.ds(2 * HD * h, HD)] = wide
-        wide = jnp.concatenate([zeros, wr[h]], axis=1)
         wd[pl.ds(2 * HD * h + HD, HD)] = wide
 
     came = pr.at[pl.ds(0, N - 1)]
@@ -148,9 +170,9 @@
     total = jnp.sum(factor * pltpu.roll(stats, 2 * HD - videos, 1), axis=0, keepdims=True)
     attended = []
     for i in range(HALF):
-        weight = jnp.where(low, factor[:, i : i + 1], factor[:, i + HALF : i + HALF + 1])
+        weight = jnp.where(low, factor[:, i + HALF : i + HALF + 1], factor[:, i : i + 1])
         accum = jnp.sum(weight * pr[:, i, :], axis=0, keepdims=True)
-        attended.append(accum / jnp.where(low, total[:, i : i + 1], total[:, i + HALF : i + HALF + 1]))
+        attended.append(accum / jnp.where(low, total[:, i + HALF : i + HALF + 1], total[:, i : i + 1]))
     att[...] = jnp.concatenate(attended, axis=0).astype(att.dtype)
 
     mine = ((yh + 1) % 2) * 4 + (x + 2) % 4
@@ -200,7 +222,7 @@
     dma = pltpu.SemaphoreType.DMA
     return pl.pallas_call(
         kernel,
-        out_shape=jax.ShapeDtypeStruct((8, videos, out_weight.shape[1]), bf16),
+        out_shape=pltpu.VMEM((8, videos, out_weight.shape[1]), bf16),
         in_specs=[anywhere] * 6,
         out_specs=pl.BlockSpec(memory_space=pltpu.VMEM),
         scratch_shapes=[
@@ -208,9 +230,9 @@
             pltpu.VMEM((1, width), f32),
             pltpu.VMEM((1, HD), bf16),
             pltpu.VMEM((2, HD, width), bf16),
-            pltpu.VMEM((2, width, 2 * HD), bf16),
-            pltpu.VMEM((tokens, width), bf16),
-            pltpu.VMEM((videos, tokens, 2 * HD), bf16),
+            pltpu.VMEM((videos, tokens, width), bf16),
+            pltpu.VMEM((HALF, 2 * HD, tokens), bf16),
+            pltpu.VMEM((HALF, tokens, 2 * HD), bf16),
             pltpu.VMEM((1, 1, 2 * HD), f32),
             pltpu.VMEM((N, 1, 2 * HD), f32),
             pltpu.VMEM((N, HALF + 1, 2 * HD), f32),

time: 46.1 us -> 41.6 us (0.902)
  Pallas kernels: 44.5 us -> 40.9 us
  local copies, waits for them, and re-layouts: 1.32 us -> 0.61 us
    pallas_call x1, Pallas kernels: 44.5 us -> 40.9 us  [per_device(): pl.pallas_call(kernel, out_shape=pltpu.VMEM((8, videos, out_weight.shape[...]
    unnamed x1, local copies, waits for them, and re-layouts: 1.32 us -> 0.61 us
where the time goes in v3:
time: 41.6 us; the launch traced here: 41.5 us
  Pallas kernels  40.9 us (98%)
  local copies, waits for them, and re-layouts  0.61 us (1%)
    pallas_call x1, Pallas kernels, per_device(): pl.pallas_call(kernel, out_shape=pltpu.VMEM((8, videos, out_weight.shape[...  40.9 us

profile of v3, /device:TPU:1, one launch (start us, length us, event | category | flops | bytes accessed | tf_op | source)
XLA Modules:
  0.0 41.5 jit_solution(8402957112888537840)
XLA Ops:
  0.0 40.9 %resampler.1 = bf16[8,8,64]{2,1,0:T(8,128)(2,1)S(1)} custom-call(bf16[8,256,1024]{2,1,0:T(8,128)(2,1)} %ctx.1, f32[1,1024]{1,0:T(1,128)} %bitcast.5, bf16[1,64]{1,0:T(2,128)(2,1)} %query.1, bf16[64,1024]{1,0:T(8,128)(2,1)} %bitcast.3, bf16[64,1024]{1,0:T(8,128)(2,1)} %bitcast.4, bf16[64,64]{1,0:T(8,128)(2,1)} %out_w.1), custom_call_target="tpu_custom_call" | custom-call | tf_op jit(solution)/shard_map/resampler/pallas_call | solution.py:223
  40.9 0.6 %copy.8 = bf16[8,8,64]{2,1,0:T(8,128)(2,1)} copy(bf16[8,8,64]{2,1,0:T(8,128)(2,1)S(1)} %resampler.1) | data formatting | bytes 16384

commit v4 on v3

--- a/solution.py
+++ b/solution.py
@@ -24,16 +24,10 @@
     return tuple((o - a) % n for o, a, n in zip(OPPOSITE, k, RING))
 
 
-def ordered_offsets():
-    every = [(a, b, c) for a in range(2) for b in range(4) for c in range(8)]
-    half = []
-    for k in sorted(every, key=lambda k: (distance(k), k)):
-        if len(half) < 32 and opposite(k) not in half:
-            half.append(k)
-    return half + [opposite(k) for k in reversed(half)]
-
-
-OFFSETS = ordered_offsets()
+EVERY = [(a, b, c) for a in range(2) for b in range(4) for c in range(8)]
+RANKS = [[k for k in EVERY if distance(k) == d] for d in range(11)]
+OFFSETS = [k for rank in RANKS for k in rank]
+SLOTS = [GROUP * d + i for d, rank in enumerate(RANKS) for i in range(len(rank))]
 N = len(OFFSETS)
 
 
@@ -58,16 +52,13 @@
         pltpu.make_async_copy(key_t, wt.at[1], in_sem.at[2]),
         pltpu.make_async_copy(gain, gbuf, in_sem.at[3]),
     ]
-    big = [pltpu.make_async_copy(ctx.at[v], xbuf.at[v], x_sem.at[v]) for v in range(videos)]
-    for copy in small:
-        copy.start()
-    big[0].start()
+    big = [pltpu.make_async_copy(ctx.at[v], xbuf.at[v], x_sem.at[v]) for v in (0, 4, 1, 5, 2, 6, 3, 7)]
     barrier = pltpu.get_barrier_semaphore()
     for k in reversed(OFFSETS[1:]):
         pl.semaphore_signal(barrier, inc=1, device_id={"tok": at(k), "head": head}, device_id_type=MESH)
     for i in range(1, 8):
         pl.semaphore_signal(barrier, inc=1, device_id={"tok": tok, "head": (head + i) % 8}, device_id_type=MESH)
-    for copy in big[1:]:
+    for copy in small + big:
         copy.start()
     own_w = pltpu.make_async_copy(out_w, wr.at[head], w_own)
     own_w.start()
@@ -78,13 +69,16 @@
     row = jnp.concatenate([row, row], axis=1)
     qs[0] = row
     qr[0] = row
+    for i in range(GROUP * len(RANKS)):
+        if i not in SLOTS:
+            qr[i] = jnp.zeros_like(row)
 
     key_value = jnp.concatenate([wt[1], wt[0]], axis=0)
     value_key = jnp.concatenate([wt[0], wt[1]], axis=0)
     low = lax.broadcasted_iota(jnp.int32, (xbuf.shape[1], 2 * HD), 1) < HD
 
     def project(v, weights):
-        big[v].wait()
+        pltpu.make_async_copy(ctx.at[v], xbuf.at[v], x_sem.at[v]).wait()
         data = xbuf[v].astype(jnp.float32)
         meansq = jnp.mean(data * data, axis=-1, keepdims=True)
         normed[v] = (data * lax.rsqrt(meansq + 1e-06) * gbuf[...]).astype(jnp.bfloat16)
@@ -97,26 +91,12 @@
         keys_t[i] = jnp.where(low, first, second).astype(jnp.bfloat16).T
         values[i] = jnp.where(low, second, first).astype(jnp.bfloat16)
 
-    pl.semaphore_wait(barrier, N - 1 + 7)
-    for j in reversed(range(1, N)):
-        pltpu.make_async_remote_copy(
-            src_ref=qs.at[0], dst_ref=qr.at[j], send_sem=q_send, recv_sem=q_recv.at[j // GROUP],
-            device_id={"tok": at(OFFSETS[j]), "head": head}, device_id_type=MESH,
-        ).start()
-    for i in range(1, 8):
-        pltpu.make_async_remote_copy(
-            src_ref=out_w, dst_ref=wr.at[head], send_sem=w_send, recv_sem=w_recv,
-            device_id={"tok": tok, "head": (head + i) % 8}, device_id_type=MESH,
-        ).start()
-
     lane = lax.broadcasted_iota(jnp.int32, (GROUP, 2 * HD), 1)
     all_keys_t = keys_t[...].reshape(HALF * 2 * HD, xbuf.shape[1])
     all_values = jnp.concatenate([values[i] for i in range(HALF)], axis=1)
-    for g in range(N // GROUP):
-        first = max(g * GROUP, 1)
-        came = qr.at[pl.ds(first, (g + 1) * GROUP - first)]
-        pltpu.make_async_copy(came, came, q_recv.at[g]).wait()
-        rows = pl.ds(g * GROUP, GROUP)
+
+    def score(d):
+        rows = pl.ds(d * GROUP, GROUP)
         both = qr[rows].reshape(GROUP, 2 * HD)
         left, right = jnp.where(lane < HD, both, 0.0), jnp.where(lane < HD, 0.0, both)
         none = jnp.zeros_like(both)
@@ -144,14 +124,35 @@
             high_rows = slice(i * GROUP, (i + 1) * GROUP)
             ps[rows, i, :] = jnp.where(lane < HD, acc[low_rows, lanes], acc[high_rows, lanes])
         ps[rows, HALF, :] = stats
-        for j in range(g * GROUP, (g + 1) * GROUP):
-            if j < N - 1:
+
+    score(0)
+    pl.semaphore_wait(barrier, N - 1 + 7)
+    for j in reversed(range(1, N)):
+        pltpu.make_async_remote_copy(
+            src_ref=qs.at[0], dst_ref=qr.at[SLOTS[j]], send_sem=q_send, recv_sem=q_recv.at[SLOTS[j] // GROUP],
+            device_id={"tok": at(OFFSETS[j]), "head": head}, device_id_type=MESH,
+        ).start()
+    for i in range(1, 8):
+        pltpu.make_async_remote_copy(
+            src_ref=out_w, dst_ref=wr.at[head], send_sem=w_send, recv_sem=w_recv,
+            device_id={"tok": tok, "head": (head + i) % 8}, device_id_type=MESH,
+        ).start()
+
+
+    for d, rank in enumerate(RANKS):
+        if d > 0:
+            came = qr.at[pl.ds(d * GROUP, len(rank))]
+            pltpu.make_async_copy(came, came, q_recv.at[d]).wait()
+            score(d)
+        for k in rank:
+            j = OFFSETS.index(k)
+            if k == OPPOSITE:
+                pr[j] = ps[SLOTS[j]]
+            else:
                 pltpu.make_async_remote_copy(
-                    src_ref=ps.at[j], dst_ref=pr.at[j], send_sem=p_send, recv_sem=p_recv,
-                    device_id={"tok": at(opposite(OFFSETS[j])), "head": head}, device_id_type=MESH,
+                    src_ref=ps.at[SLOTS[j]], dst_ref=pr.at[j], send_sem=p_send, recv_sem=p_recv,
+                    device_id={"tok": at(opposite(k)), "head": head}, device_id_type=MESH,
                 ).start()
-            else:
-                pr[j] = ps[j]
 
     own_w.wait()
     pltpu.make_async_copy(wr.at[pl.ds(0, 7)], wr.at[pl.ds(0, 7)], w_recv).wait()
@@ -234,15 +235,15 @@
             pltpu.VMEM((HALF, 2 * HD, tokens), bf16),
             pltpu.VMEM((HALF, tokens, 2 * HD), bf16),
             pltpu.VMEM((1, 1, 2 * HD), f32),
-            pltpu.VMEM((N, 1, 2 * HD), f32),
-            pltpu.VMEM((N, HALF + 1, 2 * HD), f32),
+            pltpu.VMEM((GROUP * len(RANKS), 1, 2 * HD), f32),
+            pltpu.VMEM((GROUP * len(RANKS), HALF + 1, 2 * HD), f32),
             pltpu.VMEM((N, HALF + 1, 2 * HD), f32),
             pltpu.VMEM((HALF, 2 * HD), bf16),
             pltpu.VMEM((8, 8, HALF, 2 * HD), bf16),
             pltpu.VMEM((8, HD, out_weight.shape[1]), bf16),
             pltpu.VMEM((8 * 2 * HD, 2 * HD), bf16),
             dma((4,)), dma((videos,)),
-            dma, dma((N // GROUP,)), dma, dma, dma, dma, dma, dma, dma,
+            dma, dma((len(RANKS),)), dma, dma, dma, dma, dma, dma, dma,
         ],
         compiler_params=pltpu.CompilerParams(
             collective_id=0, has_side_effects=True, vmem_limit_bytes=60 * 2**20

time: 41.6 us -> 42.4 us (1.019)
  Pallas kernels: 40.9 us -> 41.7 us
    pallas_call x1, Pallas kernels: 40.9 us -> 41.7 us  [per_device(): pl.pallas_call(kernel, out_shape=pltpu.VMEM((8, videos, out_weight.shape[...]
where the time goes in v4:
time: 42.4 us; the launch traced here: 42.3 us
  Pallas kernels  41.7 us (98%)
  local copies, waits for them, and re-layouts  0.61 us (1%)
    pallas_call x1, Pallas kernels, per_device(): pl.pallas_call(kernel, out_shape=pltpu.VMEM((8, videos, out_weight.shape[...  41.7 us

profile of v4, /device:TPU:1, one launch (start us, length us, event | category | flops | bytes accessed | tf_op | source)
XLA Modules:
  0.0 42.3 jit_solution(17512865106298301411)
XLA Ops:
  0.0 41.7 %resampler.1 = bf16[8,8,64]{2,1,0:T(8,128)(2,1)S(1)} custom-call(bf16[8,256,1024]{2,1,0:T(8,128)(2,1)} %ctx.1, f32[1,1024]{1,0:T(1,128)} %bitcast.5, bf16[1,64]{1,0:T(2,128)(2,1)} %query.1, bf16[64,1024]{1,0:T(8,128)(2,1)} %bitcast.3, bf16[64,1024]{1,0:T(8,128)(2,1)} %bitcast.4, bf16[64,64]{1,0:T(8,128)(2,1)} %out_w.1), custom_call_target="tpu_custom_call" | custom-call | tf_op jit(solution)/shard_map/resampler/pallas_call | solution.py:224
  41.7 0.6 %copy.8 = bf16[8,8,64]{2,1,0:T(8,128)(2,1)} copy(bf16[8,8,64]{2,1,0:T(8,128)(2,1)S(1)} %resampler.1) | data formatting | bytes 16384

commit v5 on v4

--- a/solution.py
+++ b/solution.py
@@ -10,6 +10,7 @@
 MESH = pl.DeviceIdType.MESH
 HD = 64
 GROUP = 8
+EARLY = 2
 HALF = 4
 RING = (2, 4, 8)
 HOPS = (4, 1, 1)
@@ -33,8 +34,8 @@
 
 def kernel(
     ctx, gain, query, key_t, value_t, out_w, out,
-    xbuf, gbuf, qin, wt, normed, keys_t, values, qs, qr, ps, pr, att, ar, wr, wd,
-    in_sem, x_sem, q_send, q_recv, p_send, p_recv, a_send, a_recv, w_send, w_recv, w_own,
+    xbuf, gbuf, qin, wt, normed, keys_t, values, qs, qr, pf, ps, pr, ss, sr, wf, att, ar, wr, wd,
+    in_sem, x_sem, q_send, q_recv, p_send, p_recv, s_send, s_recv, a_send, a_recv, w_send, w_recv, w_own,
 ):
     tok, head = lax.axis_index("tok"), lax.axis_index("head")
     yh, x, z = tok // 32, (tok // 8) % 4, tok % 8
@@ -53,15 +54,15 @@
         pltpu.make_async_copy(gain, gbuf, in_sem.at[3]),
     ]
     big = [pltpu.make_async_copy(ctx.at[v], xbuf.at[v], x_sem.at[v]) for v in (0, 4, 1, 5, 2, 6, 3, 7)]
+    for copy in small + big:
+        copy.start()
+    own_w = pltpu.make_async_copy(out_w, wr.at[head], w_own)
+    own_w.start()
     barrier = pltpu.get_barrier_semaphore()
     for k in reversed(OFFSETS[1:]):
         pl.semaphore_signal(barrier, inc=1, device_id={"tok": at(k), "head": head}, device_id_type=MESH)
     for i in range(1, 8):
         pl.semaphore_signal(barrier, inc=1, device_id={"tok": tok, "head": (head + i) % 8}, device_id_type=MESH)
-    for copy in small + big:
-        copy.start()
-    own_w = pltpu.make_async_copy(out_w, wr.at[head], w_own)
-    own_w.start()
 
     for copy in small:
         copy.wait()
@@ -86,10 +87,25 @@
             normed[v], weights, (((1,), (1,)), ((), ())), preferred_element_type=jnp.float32
         )
 
-    for i in range(HALF):
-        first, second = project(i, key_value), project(i + HALF, value_key)
-        keys_t[i] = jnp.where(low, first, second).astype(jnp.bfloat16).T
-        values[i] = jnp.where(low, second, first).astype(jnp.bfloat16)
+    def project_pairs(pairs):
+        for i in pairs:
+            first, second = project(i, key_value), project(i + HALF, value_key)
+            keys_t[i] = jnp.where(low, first, second).astype(jnp.bfloat16).T
+            values[i] = jnp.where(low, second, first).astype(jnp.bfloat16)
+
+    project_pairs(range(EARLY))
+    pl.semaphore_wait(barrier, N - 1 + 7)
+    for j in reversed(range(1, N)):
+        pltpu.make_async_remote_copy(
+            src_ref=qs.at[0], dst_ref=qr.at[SLOTS[j]], send_sem=q_send, recv_sem=q_recv.at[SLOTS[j] // GROUP],
+            device_id={"tok": at(OFFSETS[j]), "head": head}, device_id_type=MESH,
+        ).start()
+    for i in range(1, 8):
+        pltpu.make_async_remote_copy(
+            src_ref=out_w, dst_ref=wr.at[head], send_sem=w_send, recv_sem=w_recv,
+            device_id={"tok": tok, "head": (head + i) % 8}, device_id_type=MESH,
+        ).start()
+    project_pairs(range(EARLY, HALF))
 
     lane = lax.broadcasted_iota(jnp.int32, (GROUP, 2 * HD), 1)
     all_keys_t = keys_t[...].reshape(HALF * 2 * HD, xbuf.shape[1])
@@ -122,23 +138,11 @@
             lanes = slice(2 * HD * i, 2 * HD * (i + 1))
             low_rows = slice((i + HALF) * GROUP, (i + HALF + 1) * GROUP)
             high_rows = slice(i * GROUP, (i + 1) * GROUP)
-            ps[rows, i, :] = jnp.where(lane < HD, acc[low_rows, lanes], acc[high_rows, lanes])
-        ps[rows, HALF, :] = stats
+            pf[rows, i, :] = jnp.where(lane < HD, acc[low_rows, lanes], acc[high_rows, lanes])
+        ps[rows] = pf[rows].astype(jnp.bfloat16)
+        ss[rows] = stats.reshape(GROUP, 1, 2 * HD)
 
     score(0)
-    pl.semaphore_wait(barrier, N - 1 + 7)
-    for j in reversed(range(1, N)):
-        pltpu.make_async_remote_copy(
-            src_ref=qs.at[0], dst_ref=qr.at[SLOTS[j]], send_sem=q_send, recv_sem=q_recv.at[SLOTS[j] // GROUP],
-            device_id={"tok": at(OFFSETS[j]), "head": head}, device_id_type=MESH,
-        ).start()
-    for i in range(1, 8):
-        pltpu.make_async_remote_copy(
-            src_ref=out_w, dst_ref=wr.at[head], send_sem=w_send, recv_sem=w_recv,
-            device_id={"tok": tok, "head": (head + i) % 8}, device_id_type=MESH,
-        ).start()
-
-
     for d, rank in enumerate(RANKS):
         if d > 0:
             came = qr.at[pl.ds(d * GROUP, len(rank))]
@@ -148,7 +152,12 @@
             j = OFFSETS.index(k)
             if k == OPPOSITE:
                 pr[j] = ps[SLOTS[j]]
+                sr[j] = ss[SLOTS[j]]
             else:
+                pltpu.make_async_remote_copy(
+                    src_ref=ss.at[SLOTS[j]], dst_ref=sr.at[j], send_sem=s_send, recv_sem=s_recv,
+                    device_id={"tok": at(opposite(k)), "head": head}, device_id_type=MESH,
+                ).start()
                 pltpu.make_async_remote_copy(
                     src_ref=ps.at[SLOTS[j]], dst_ref=pr.at[j], send_sem=p_send, recv_sem=p_recv,
                     device_id={"tok": at(opposite(k)), "head": head}, device_id_type=MESH,
@@ -163,18 +172,20 @@
         wide = jnp.concatenate([wr[h], zeros], axis=1)
         wd[pl.ds(2 * HD * h + HD, HD)] = wide
 
-    came = pr.at[pl.ds(0, N - 1)]
-    pltpu.make_async_copy(came, came, p_recv).wait()
-    stats = pr[:, HALF, :]
+    came = sr.at[pl.ds(0, N - 1)]
+    pltpu.make_async_copy(came, came, s_recv).wait()
+    stats = sr[...].reshape(N, 2 * HD)
     low = lax.broadcasted_iota(jnp.int32, (1, 2 * HD), 1) < HD
     factor = jnp.exp(stats - jnp.max(stats, axis=0, keepdims=True))
     total = jnp.sum(factor * pltpu.roll(stats, 2 * HD - videos, 1), axis=0, keepdims=True)
-    attended = []
+    totals = []
     for i in range(HALF):
-        weight = jnp.where(low, factor[:, i + HALF : i + HALF + 1], factor[:, i : i + 1])
-        accum = jnp.sum(weight * pr[:, i, :], axis=0, keepdims=True)
-        attended.append(accum / jnp.where(low, total[:, i + HALF : i + HALF + 1], total[:, i : i + 1]))
-    att[...] = jnp.concatenate(attended, axis=0).astype(att.dtype)
+        wf[:, i, :] = jnp.where(low, factor[:, i + HALF : i + HALF + 1], factor[:, i : i + 1])
+        totals.append(jnp.where(low, total[:, i + HALF : i + HALF + 1], total[:, i : i + 1]))
+    came = pr.at[pl.ds(0, N - 1)]
+    pltpu.make_async_copy(came, came, p_recv).wait()
+    accum = jnp.sum(wf[...] * pr[...].astype(jnp.float32), axis=0)
+    att[...] = (accum / jnp.concatenate(totals, axis=0)).astype(att.dtype)
 
     mine = ((yh + 1) % 2) * 4 + (x + 2) % 4
     slot = (z + 4) % 8
@@ -200,6 +211,8 @@
     pltpu.make_async_copy(gone, gone, q_send).wait()
     gone = ps.at[pl.ds(0, N - 1)]
     pltpu.make_async_copy(gone, gone, p_send).wait()
+    gone = ss.at[pl.ds(0, N - 1)]
+    pltpu.make_async_copy(gone, gone, s_send).wait()
 
     pltpu.make_async_copy(ar, ar, a_recv).wait()
     blocks = [ar[h].astype(jnp.float32).reshape(8 * HALF, 2 * HD).astype(jnp.bfloat16) for h in range(8)]
@@ -236,14 +249,18 @@
             pltpu.VMEM((HALF, tokens, 2 * HD), bf16),
             pltpu.VMEM((1, 1, 2 * HD), f32),
             pltpu.VMEM((GROUP * len(RANKS), 1, 2 * HD), f32),
-            pltpu.VMEM((GROUP * len(RANKS), HALF + 1, 2 * HD), f32),
-            pltpu.VMEM((N, HALF + 1, 2 * HD), f32),
+            pltpu.VMEM((GROUP * len(RANKS), HALF, 2 * HD), f32),
+            pltpu.VMEM((GROUP * len(RANKS), HALF, 2 * HD), bf16),
+            pltpu.VMEM((N, HALF, 2 * HD), bf16),
+            pltpu.VMEM((GROUP * len(RANKS), 1, 2 * HD), f32),
+            pltpu.VMEM((N, 1, 2 * HD), f32),
+            pltpu.VMEM((N, HALF, 2 * HD), f32),
             pltpu.VMEM((HALF, 2 * HD), bf16),
             pltpu.VMEM((8, 8, HALF, 2 * HD), bf16),
             pltpu.VMEM((8, HD, out_weight.shape[1]), bf16),
             pltpu.VMEM((8 * 2 * HD, 2 * HD), bf16),
             dma((4,)), dma((videos,)),
-            dma, dma((len(RANKS),)), dma, dma, dma, dma, dma, dma, dma,
+            dma, dma((len(RANKS),)), dma, dma, dma, dma, dma, dma, dma, dma, dma,
         ],
         compiler_params=pltpu.CompilerParams(
             collective_id=0, has_side_effects=True, vmem_limit_bytes=60 * 2**20

time: 42.4 us -> 41.4 us (0.976)
  Pallas kernels: 41.7 us -> 40.7 us
    pallas_call x1, Pallas kernels: 41.7 us -> 40.7 us  [per_device(): pl.pallas_call(kernel, out_shape=pltpu.VMEM((8, videos, out_weight.shape[...]
where the time goes in v5:
time: 41.4 us; the launch traced here: 41.3 us
  Pallas kernels  40.7 us (98%)
  local copies, waits for them, and re-layouts  0.61 us (1%)
    pallas_call x1, Pallas kernels, per_device(): pl.pallas_call(kernel, out_shape=pltpu.VMEM((8, videos, out_weight.shape[...  40.7 us

profile of v5, /device:TPU:1, one launch (start us, length us, event | category | flops | bytes accessed | tf_op | source)
XLA Modules:
  0.0 41.3 jit_solution(4720684978193473523)
XLA Ops:
  0.0 40.7 %resampler.1 = bf16[8,8,64]{2,1,0:T(8,128)(2,1)S(1)} custom-call(bf16[8,256,1024]{2,1,0:T(8,128)(2,1)} %ctx.1, f32[1,1024]{1,0:T(1,128)} %bitcast.5, bf16[1,64]{1,0:T(2,128)(2,1)} %query.1, bf16[64,1024]{1,0:T(8,128)(2,1)} %bitcast.3, bf16[64,1024]{1,0:T(8,128)(2,1)} %bitcast.4, bf16[64,64]{1,0:T(8,128)(2,1)} %out_w.1), custom_call_target="tpu_custom_call" | custom-call | tf_op jit(solution)/shard_map/resampler/pallas_call | solution.py:237
  40.7 0.6 %copy.8 = bf16[8,8,64]{2,1,0:T(8,128)(2,1)} copy(bf16[8,8,64]{2,1,0:T(8,128)(2,1)S(1)} %resampler.1) | data formatting | bytes 16384

commit v6 on v4

--- a/solution.py
+++ b/solution.py
@@ -10,6 +10,7 @@
 MESH = pl.DeviceIdType.MESH
 HD = 64
 GROUP = 8
+EARLY = 2
 HALF = 4
 RING = (2, 4, 8)
 HOPS = (4, 1, 1)
@@ -27,6 +28,7 @@
 EVERY = [(a, b, c) for a in range(2) for b in range(4) for c in range(8)]
 RANKS = [[k for k in EVERY if distance(k) == d] for d in range(11)]
 OFFSETS = [k for rank in RANKS for k in rank]
+RANKS = [OFFSETS[:1]] + [OFFSETS[i : i + GROUP] for i in range(1, len(OFFSETS), GROUP)]
 SLOTS = [GROUP * d + i for d, rank in enumerate(RANKS) for i in range(len(rank))]
 N = len(OFFSETS)
 
@@ -53,15 +55,15 @@
         pltpu.make_async_copy(gain, gbuf, in_sem.at[3]),
     ]
     big = [pltpu.make_async_copy(ctx.at[v], xbuf.at[v], x_sem.at[v]) for v in (0, 4, 1, 5, 2, 6, 3, 7)]
+    for copy in small + big:
+        copy.start()
+    own_w = pltpu.make_async_copy(out_w, wr.at[head], w_own)
+    own_w.start()
     barrier = pltpu.get_barrier_semaphore()
     for k in reversed(OFFSETS[1:]):
         pl.semaphore_signal(barrier, inc=1, device_id={"tok": at(k), "head": head}, device_id_type=MESH)
     for i in range(1, 8):
         pl.semaphore_signal(barrier, inc=1, device_id={"tok": tok, "head": (head + i) % 8}, device_id_type=MESH)
-    for copy in small + big:
-        copy.start()
-    own_w = pltpu.make_async_copy(out_w, wr.at[head], w_own)
-    own_w.start()
 
     for copy in small:
         copy.wait()
@@ -86,10 +88,25 @@
             normed[v], weights, (((1,), (1,)), ((), ())), preferred_element_type=jnp.float32
         )
 
-    for i in range(HALF):
-        first, second = project(i, key_value), project(i + HALF, value_key)
-        keys_t[i] = jnp.where(low, first, second).astype(jnp.bfloat16).T
-        values[i] = jnp.where(low, second, first).astype(jnp.bfloat16)
+    def project_pairs(pairs):
+        for i in pairs:
+            first, second = project(i, key_value), project(i + HALF, value_key)
+            keys_t[i] = jnp.where(low, first, second).astype(jnp.bfloat16).T
+            values[i] = jnp.where(low, second, first).astype(jnp.bfloat16)
+
+    project_pairs(range(EARLY))
+    pl.semaphore_wait(barrier, N - 1 + 7)
+    for j in [j for pair in zip(reversed(range(32, N)), range(1, 32)) for j in pair] + [32]:
+        pltpu.make_async_remote_copy(
+            src_ref=qs.at[0], dst_ref=qr.at[SLOTS[j]], send_sem=q_send, recv_sem=q_recv.at[SLOTS[j] // GROUP],
+            device_id={"tok": at(OFFSETS[j]), "head": head}, device_id_type=MESH,
+        ).start()
+    for i in range(1, 8):
+        pltpu.make_async_remote_copy(
+            src_ref=out_w, dst_ref=wr.at[head], send_sem=w_send, recv_sem=w_recv,
+            device_id={"tok": tok, "head": (head + i) % 8}, device_id_type=MESH,
+        ).start()
+    project_pairs(range(EARLY, HALF))
 
     lane = lax.broadcasted_iota(jnp.int32, (GROUP, 2 * HD), 1)
     all_keys_t = keys_t[...].reshape(HALF * 2 * HD, xbuf.shape[1])
@@ -126,19 +143,6 @@
         ps[rows, HALF, :] = stats
 
     score(0)
-    pl.semaphore_wait(barrier, N - 1 + 7)
-    for j in reversed(range(1, N)):
-        pltpu.make_async_remote_copy(
-            src_ref=qs.at[0], dst_ref=qr.at[SLOTS[j]], send_sem=q_send, recv_sem=q_recv.at[SLOTS[j] // GROUP],
-            device_id={"tok": at(OFFSETS[j]), "head": head}, device_id_type=MESH,
-        ).start()
-    for i in range(1, 8):
-        pltpu.make_async_remote_copy(
-            src_ref=out_w, dst_ref=wr.at[head], send_sem=w_send, recv_sem=w_recv,
-            device_id={"tok": tok, "head": (head + i) % 8}, device_id_type=MESH,
-        ).start()
-
-
     for d, rank in enumerate(RANKS):
         if d > 0:
             came = qr.at[pl.ds(d * GROUP, len(rank))]

time: 42.4 us -> 41.5 us (0.979)
  Pallas kernels: 41.7 us -> 40.8 us
    pallas_call x1, Pallas kernels: 41.7 us -> 40.8 us  [per_device(): pl.pallas_call(kernel, out_shape=pltpu.VMEM((8, videos, out_weight.shape[...]
where the time goes in v6:
time: 41.5 us; the launch traced here: 41.4 us
  Pallas kernels  40.8 us (98%)
  local copies, waits for them, and re-layouts  0.61 us (1%)
    pallas_call x1, Pallas kernels, per_device(): pl.pallas_call(kernel, out_shape=pltpu.VMEM((8, videos, out_weight.shape[...  40.8 us

profile of v6, /device:TPU:1, one launch (start us, length us, event | category | flops | bytes accessed | tf_op | source)
XLA Modules:
  0.0 41.4 jit_solution(16660238196410797967)
XLA Ops:
  0.0 40.8 %resampler.1 = bf16[8,8,64]{2,1,0:T(8,128)(2,1)S(1)} custom-call(bf16[8,256,1024]{2,1,0:T(8,128)(2,1)} %ctx.1, f32[1,1024]{1,0:T(1,128)} %bitcast.5, bf16[1,64]{1,0:T(2,128)(2,1)} %query.1, bf16[64,1024]{1,0:T(8,128)(2,1)} %bitcast.3, bf16[64,1024]{1,0:T(8,128)(2,1)} %bitcast.4, bf16[64,64]{1,0:T(8,128)(2,1)} %out_w.1), custom_call_target="tpu_custom_call" | custom-call | tf_op jit(solution)/shard_map/resampler/pallas_call | solution.py:228
  40.8 0.6 %copy.8 = bf16[8,8,64]{2,1,0:T(8,128)(2,1)} copy(bf16[8,8,64]{2,1,0:T(8,128)(2,1)S(1)} %resampler.1) | data formatting | bytes 16384

commit v7 on v6

--- a/solution.py
+++ b/solution.py
@@ -41,8 +41,9 @@
     tok, head = lax.axis_index("tok"), lax.axis_index("head")
     yh, x, z = tok // 32, (tok // 8) % 4, tok % 8
     ys = [((yh + a) % 2) * 32 for a in range(2)]
-    xs = [((x + a) % 4) * 8 for a in range(4)]
-    zs = [(z + a) % 8 for a in range(8)]
+    way = 1 - 2 * (head % 2)
+    xs = [((x + 4 + way * a) % 4) * 8 for a in range(4)]
+    zs = [(z + 8 + way * a) % 8 for a in range(8)]
 
     def at(k):
         return ys[k[0]] + xs[k[1]] + zs[k[2]]

time: 41.5 us -> 41.7 us (level)
  no operation moved by 1% of the time
where the time goes in v7:
time: 41.7 us; the launch traced here: 41.6 us
  Pallas kernels  41 us (98%)
  local copies, waits for them, and re-layouts  0.61 us (1%)
    pallas_call x1, Pallas kernels, per_device(): pl.pallas_call(kernel, out_shape=pltpu.VMEM((8, videos, out_weight.shape[...  41 us

profile of v7, /device:TPU:1, one launch (start us, length us, event | category | flops | bytes accessed | tf_op | source)
XLA Modules:
  0.0 41.6 jit_solution(1007386470750446278)
XLA Ops:
  0.0 41.0 %resampler.1 = bf16[8,8,64]{2,1,0:T(8,128)(2,1)S(1)} custom-call(bf16[8,256,1024]{2,1,0:T(8,128)(2,1)} %ctx.1, f32[1,1024]{1,0:T(1,128)} %bitcast.5, bf16[1,64]{1,0:T(2,128)(2,1)} %query.1, bf16[64,1024]{1,0:T(8,128)(2,1)} %bitcast.3, bf16[64,1024]{1,0:T(8,128)(2,1)} %bitcast.4, bf16[64,64]{1,0:T(8,128)(2,1)} %out_w.1), custom_call_target="tpu_custom_call" | custom-call | tf_op jit(solution)/shard_map/resampler/pallas_call | solution.py:229
  41.0 0.6 %copy.8 = bf16[8,8,64]{2,1,0:T(8,128)(2,1)} copy(bf16[8,8,64]{2,1,0:T(8,128)(2,1)S(1)} %resampler.1) | data formatting | bytes 16384
